TPU v7x, 32 devices: a whole 2x2x4 slice. The times are simulated.
32 devices in a mesh: dp: 8 (over z, core), tensor: 4 (over y, x).
Axes of the slice: x: 2, y: 2, z: 4, core: 2. Of those that a mesh axis runs over, the one named last changes fastest.
Arguments:
- features: bfloat16 [2560, 2048], P(('dp', 'tensor')), may hold values from -6 to 6
- w_hidden: bfloat16 [2048, 2048], P(None, 'tensor'), may hold values from -0.125 to 0.125
- w_embed: bfloat16 [2048, 768], P('tensor'), may hold values from -0.125 to 0.125
- members: bfloat16 [8, 512, 768], P('dp', 'tensor'), may hold values from -6 to 6
- doc_owner: int32 [2560, 1], P('dp'), may hold values from 0 to 7; in each aligned block of 80 rows (0 to 79, 80 to 159, ...) at most 20 rows name the same one
- doc_local: int32 [2560], P('dp'), may hold values from 0 to 15
- member_cluster: int32 [8, 512], P('dp', 'tensor'), may hold values from 0 to 15, never falling along the last dimension, each value on 1 to 48 neighbouring positions
- member_valid: int32 [8, 512], P('dp', 'tensor'), may hold values 0 or 1
Outputs:
- best: float32 [2560], P(('dp', 'tensor'))
Inputs may be any that keep to these rules, and one draw needn't show every extreme that they name: Among the 80 documents of one device (aligned blocks of doc_owner's rows, in the order of dp then tensor) no owner is named more than 20 times; some owner is named exactly 20 times. `member_cluster`: along each owner's row the clusters never fall; every cluster has 1 to 48 slots.
All inputs are finite; a program needn't handle non-finite values. No bound on the sum of `member_valid` on one device may be relied on, other than what follows from the above.
Results may differ from a plain program's by a relative error of at most 0.013.
Values may be sent and summed in bfloat16 or wider, within the bound.
A program may use at most 64 MiB of HBM per device.

v0:
```python
import jax
import jax.numpy as jnp
from jax import lax
from jax.sharding import PartitionSpec as P

epsilon = 1e-06


def unit_rows(vectors):
    values = vectors.astype(jnp.float32)
    return (values / jnp.sqrt(jnp.sum(values * values, axis=-1, keepdims=True) + epsilon)).astype(
        jnp.bfloat16
    )


def slot_of(owner, owners_count, slot_cap):
    onehot = (owner[:, None] == jnp.arange(owners_count, dtype=jnp.int32)[None, :]).astype(
        jnp.int32
    )
    ranking = jnp.sum((jnp.cumsum(onehot, axis=0) - 1) * onehot, axis=1)
    return owner * slot_cap + ranking


def pack_rows(query, local, slot_index, slot_total):
    placing = slot_index[None, :] == jnp.arange(slot_total, dtype=jnp.int32)[:, None]
    outgoing = jnp.dot(
        placing.astype(jnp.bfloat16), query, preferred_element_type=jnp.float32
    ).astype(jnp.bfloat16)
    slot_tag = jnp.sum(jnp.where(placing, local[None, :] + 1, 0), axis=1)
    return (outgoing, slot_tag)


def best_scores(arrived, arrived_tag, unit, cluster_here, valid_here):
    scores = lax.dot_general(
        arrived, unit, (((1,), (1,)), ((), ())), preferred_element_type=jnp.float32
    )
    allowed = (valid_here[None, :] == 1) & (cluster_here[None, :] == arrived_tag[:, None] - 1)
    return jnp.max(jnp.where(allowed, scores, -1.0), axis=1)


def body(features, w_hidden, w_embed, members, doc_owner, doc_local, member_cluster, member_valid):
    owners_count = lax.axis_size("dp")
    tensor_index = lax.axis_index("tensor")
    row_total = features.shape[0]
    slot_cap = min(row_total, max(2, 2 * row_total // owners_count))
    hidden = jax.nn.gelu(
        jnp.dot(
            lax.all_gather(features, "tensor", axis=0, tiled=True),
            w_hidden,
            preferred_element_type=jnp.float32,
        )
    ).astype(jnp.bfloat16)
    unit = unit_rows(members.reshape(members.shape[1], members.shape[2]))
    cluster_here = member_cluster.reshape(-1)
    valid_here = member_valid.reshape(-1)
    owner_all = doc_owner[:, 0]
    summed = lax.psum_scatter(
        jnp.dot(hidden, w_embed, preferred_element_type=jnp.float32).astype(jnp.bfloat16),
        "tensor",
        scatter_dimension=0,
        tiled=True,
    ).astype(jnp.float32)
    query = unit_rows(summed)
    owner = lax.dynamic_slice_in_dim(owner_all, tensor_index * row_total, row_total, 0)
    local = lax.dynamic_slice_in_dim(doc_local, tensor_index * row_total, row_total, 0)
    slot_total = owners_count * slot_cap
    slot_index = slot_of(owner, owners_count, slot_cap)
    outgoing, slot_tag = pack_rows(query, local, slot_index, slot_total)
    arrived, arrived_tag = (
        lax.all_to_all(outgoing, "dp", split_axis=0, concat_axis=0, tiled=True),
        lax.all_to_all(slot_tag, "dp", split_axis=0, concat_axis=0, tiled=True),
    )
    shared, shared_tag = (
        lax.all_gather(arrived, "tensor", axis=0, tiled=True),
        lax.all_gather(arrived_tag, "tensor", axis=0, tiled=True),
    )
    partial_value = best_scores(shared, shared_tag, unit, cluster_here, valid_here)
    merged = lax.pmax(partial_value, "tensor")
    own_best = lax.dynamic_slice_in_dim(merged, tensor_index * slot_total, slot_total, 0)
    answers = lax.all_to_all(own_best, "dp", split_axis=0, concat_axis=0, tiled=True)
    return jnp.take(answers, slot_index, axis=0)


def solution(mesh):
    return jax.shard_map(
        body,
        mesh=mesh,
        in_specs=(
            P(("dp", "tensor"), None),
            P(None, "tensor"),
            P("tensor", None),
            P("dp", "tensor", None),
            P("dp", None),
            P("dp"),
            P("dp", "tensor"),
            P("dp", "tensor"),
        ),
        out_specs=P(("dp", "tensor")),
        check_vma=False,
    )
```

profile of v0, /device:TPU:0, one launch (start us, length us, event | category | flops | bytes accessed | tf_op | source)
XLA Modules:
  0.0 128.8 jit_solution(12317580258598215168)
XLA Ops:
  6.5 0.0 copy-start
  6.5 0.7 all-gather.2.cloned.1.call-update
  7.3 0.0 reduce-scatter.2.cloned.1.call-start
  7.3 0.8 fusion.25
  8.1 0.1 fusion.24
  8.2 0.1 reduce_window_sum.11
  8.3 0.2 select_reduce_fusion.1
  8.4 0.0 copy-start.2
  8.5 0.0 copy-start.5
  8.5 0.0 copy-start.1
  8.5 32.3 %all-gather.2.cloned.1.call-done = bf16[320,2048]{1,0:T(8,128)(2,1)} async-done(((bf16[80,2048]{1,0:T(8,128)(2,1)}), bf16[320,2048]{1,0:T(8,128)(2,1)}) %all-gather.2.cloned.1.call-update) | async-done | bytes 1310736 | tf_op jit(solution)/shard_map/all_gather | solution.py:48
  40.7 0.0 copy-done
  40.7 3.6 %convolution_convert_fusion = bf16[320,768]{1,0:T(8,128)(2,1)} fusion(bf16[512,768]{1,0:T(8,128)(2,1)} %param.10, bf16[320,2048]{1,0:T(8,128)(2,1)} %all-gather.2.cloned.1.call-done, bf16[2048,512]{1,0:T(8,128)(2,1)S(1)} %copy-done), kind=kOutput, calls=%fused_computation.1 | convolution fusion | flops 924467200 | bytes 4685824 | tf_op jit(solution)/shard_map/dot_general | solution.py:58
  44.3 0.0 reduce-scatter.2.cloned.1.call-update
  44.4 0.8 dynamic-slice_add_fusion
  45.1 0.1 multiply_add_fusion
  45.2 0.1 select_reduce_fusion
  45.3 0.7 all_to_all.24
  46.0 4.6 %all-to-all-start = ((s32[8,20,1]{1,2,0:T(1,128)}), s32[8,20,1]{1,2,0:T(1,128)S(1)}, u32[]{:S(2)}, u32[]{:S(2)}) async-start(s32[8,20,1]{1,2,0:T(1,128)} %bitcast.5), calls=%async_computation | async-start | bytes 8192 | tf_op jit(solution)/shard_map/all_to_all | solution.py:71
  50.6 0.6 dynamic-slice.1
  51.9 0.0 copy-start.4
  51.9 0.1 fusion.9
  52.0 0.1 compare_select_fusion
  52.1 17.1 %reduce-scatter.2.cloned.1.call-done = bf16[80,768]{1,0:T(8,128)(2,1)} async-done(((bf16[320,768]{1,0:T(8,128)(2,1)}), bf16[80,768]{1,0:T(8,128)(2,1)}) %reduce-scatter.2.cloned.1.call-update) | async-done | bytes 122896 | tf_op jit(solution)/shard_map/reduce_scatter | solution.py:57
  69.2 1.0 fusion.16
  70.3 1.2 convolution_convert_fusion.1
  71.5 0.8 all_to_all.27
  72.2 0.0 all-to-all-done
  72.2 4.6 %all-to-all-start.1 = ((bf16[8,20,768]{2,1,0:T(8,128)(2,1)}), bf16[8,20,768]{2,1,0:T(8,128)(2,1)S(1)}, u32[]{:S(2)}, u32[]{:S(2)}) async-start(bf16[8,20,768]{2,1,0:T(8,128)(2,1)} %all_to_all.27), calls=%async_computation.2 | async-start | bytes 589824 | tf_op jit(solution)/shard_map/all_to_all | solution.py:70
  76.9 0.5 broadcast.54
  77.4 0.7 reduce.6
  78.1 0.1 reshape.50
  78.1 0.2 dynamic-update-slice
  78.4 7.3 %all-reduce = s32[640]{0:T(1024)S(1)} all-reduce(s32[640]{0:T(1024)S(1)} %dynamic-update-slice), channel_id=1, replica_groups=mesh['dp'=8,'tensor'=4] {'tensor'}, use_global_device_ids=true, to_apply=%add | all-reduce | flops 640 | bytes 5120
  85.7 1.6 %all-to-all-done.1 = bf16[8,20,768]{2,1,0:T(8,128)(2,1)S(1)} async-done(((bf16[8,20,768]{2,1,0:T(8,128)(2,1)}), bf16[8,20,768]{2,1,0:T(8,128)(2,1)S(1)}, u32[]{:S(2)}, u32[]{:S(2)}) %all-to-all-start.1) | async-done | bytes 245792 | tf_op jit(solution)/shard_map/all_to_all | solution.py:70
  87.3 0.1 all_to_all.29
  87.4 12.1 %all_gather.11 = bf16[640,768]{1,0:T(8,128)(2,1)S(1)} all-gather(bf16[160,768]{1,0:T(8,128)(2,1)S(1)} %all_to_all.29), channel_id=1, replica_groups=mesh['dp'=8,'tensor'=4] {'tensor'}, dimensions={0}, use_global_device_ids=true | all-gather | bytes 1228800 | tf_op jit(solution)/shard_map/all_gather | solution.py:74
  99.4 0.5 fusion
  99.9 8.9 %pmax.7 = f32[640]{0:T(1024)S(1)} all-reduce(f32[640]{0:T(1024)S(1)} %fusion), channel_id=1, replica_groups=mesh['dp'=8,'tensor'=4] {'tensor'}, use_global_device_ids=true, to_apply=%region_7.8 | all-reduce | flops 640 | bytes 5120 | tf_op jit(solution)/shard_map/pmax | solution.py:78
  108.8 0.1 dynamic_slice.11
  108.9 0.7 all_to_all.30
  109.6 3.7 %all-to-all-start.2 = ((f32[8,20,1]{1,2,0:T(1,128)}), f32[8,20,1]{1,2,0:T(1,128)S(1)}, u32[]{:S(2)}, u32[]{:S(2)}) async-start(f32[8,20,1]{1,2,0:T(1,128)} %bitcast.9), calls=%async_computation.3 | async-start | bytes 8192 | tf_op jit(solution)/shard_map/all_to_all | solution.py:80
  113.3 5.5 %all-to-all-done.2 = f32[8,20,1]{1,2,0:T(1,128)S(1)} async-done(((f32[8,20,1]{1,2,0:T(1,128)}), f32[8,20,1]{1,2,0:T(1,128)S(1)}, u32[]{:S(2)}, u32[]{:S(2)}) %all-to-all-start.2) | async-done | bytes 672 | tf_op jit(solution)/shard_map/all_to_all | solution.py:80
  118.9 0.5 broadcast.55
  119.4 0.7 reduce.7
  120.1 0.1 all_to_all.32
  120.1 1.3 gather_fusion
  121.4 0.5 bitcast_select_fusion
  (13 shorter events, 0.0 us)
Async XLA Ops:
  6.5 34.2 %copy-start = (bf16[2048,512]{1,0:T(8,128)(2,1)S(1)}, bf16[2048,512]{1,0:T(8,128)(2,1)}, u32[]{:S(2)}) copy-start(bf16[2048,512]{1,0:T(8,128)(2,1)} %param.9) | copy-start | bytes 6291460
  6.5 34.2 %all-gather.2.cloned.1.call-start = ((), (), s32[]{:S(2)}) async-start(), calls=%async_computation.4 | async-start | bytes 1638400 | tf_op jit(solution)/shard_map/all_gather | solution.py:48
  7.3 62.0 %reduce-scatter.2.cloned.1.call-start = ((), (), s32[]{:S(2)}) async-start(), calls=%async_computation.5 | async-start | bytes 614400 | tf_op jit(solution)/shard_map/reduce_scatter | solution.py:57
  8.4 36.7 %copy-start.2 = (s32[320,1]{0,1:T(1,128)S(1)}, s32[320,1]{0,1:T(1,128)}, u32[]{:S(2)}) copy-start(s32[320,1]{0,1:T(1,128)} %param.12) | copy-start | bytes 3844
  8.5 42.2 %copy-start.5 = (u32[32]{0:T(128)S(1)}, u32[32]{0:T(128)}, u32[]{:S(2)}) copy-start(u32[32]{0:T(128)} %constant.66) | copy-start | bytes 388
  8.5 43.4 %copy-start.1 = (bf16[1,128,768]{2,1,0:T(8,128)(2,1)S(1)}, bf16[1,128,768]{2,1,0:T(8,128)(2,1)}, u32[]{:S(2)}) copy-start(bf16[1,128,768]{2,1,0:T(8,128)(2,1)} %param.11) | copy-start | bytes 589828
  44.3 32.5 %copy-start.3 = (s32[1,128]{1,0:T(1,128)S(1)}, s32[1,128]{1,0:T(1,128)}, u32[]{:S(2)}) copy-start(s32[1,128]{1,0:T(1,128)} %param.15) | copy-start | bytes 1540
  46.0 26.2 %all-to-all-start = ((s32[8,20,1]{1,2,0:T(1,128)}), s32[8,20,1]{1,2,0:T(1,128)S(1)}, u32[]{:S(2)}, u32[]{:S(2)}) async-start(s32[8,20,1]{1,2,0:T(1,128)} %bitcast.5), calls=%async_computation | async-start | bytes 8192 | tf_op jit(solution)/shard_map/all_to_all | solution.py:71
  51.9 47.6 %copy-start.4 = (s32[1,128]{1,0:T(1,128)S(1)}, s32[1,128]{1,0:T(1,128)}, u32[]{:S(2)}) copy-start(s32[1,128]{1,0:T(1,128)} %param.14) | copy-start | bytes 1540
  72.2 15.1 %all-to-all-start.1 = ((bf16[8,20,768]{2,1,0:T(8,128)(2,1)}), bf16[8,20,768]{2,1,0:T(8,128)(2,1)S(1)}, u32[]{:S(2)}, u32[]{:S(2)}) async-start(bf16[8,20,768]{2,1,0:T(8,128)(2,1)} %all_to_all.27), calls=%async_computation.2 | async-start | bytes 589824 | tf_op jit(solution)/shard_map/all_to_all | solution.py:70
  109.6 9.3 %all-to-all-start.2 = ((f32[8,20,1]{1,2,0:T(1,128)}), f32[8,20,1]{1,2,0:T(1,128)S(1)}, u32[]{:S(2)}, u32[]{:S(2)}) async-start(f32[8,20,1]{1,2,0:T(1,128)} %bitcast.9), calls=%async_computation.3 | async-start | bytes 8192 | tf_op jit(solution)/shard_map/all_to_all | solution.py:80
Sparse Core Ops, SparseCore 0:
  9.2 31.4 all-gather.1
  44.5 24.6 reduce-scatter.1
where the time goes:
time: 129 us
  waiting for transfers between devices  57.3 us (44%)
  blocking collectives  28.3 us (22%)
  between operations  14.2 us (11%)
  starting transfers between devices  13 us (10%)
  local copies, waits for them, and re-layouts  6.32 us (5%)
  matrix products  5.25 us (4%)
  other arithmetic  4.4 us (3%)
    all_gather x1, waiting for transfers between devices, body(): lax.all_gather(features, 'tensor', axis=0, tiled=True)  32.3 us
    reduce_scatter x1, waiting for transfers between devices, body(): lax.psum_scatter(jnp.dot(hidden, w_embed, preferred_element_type=jnp.floa...  17.1 us
    all_gather x1, blocking collectives, body(): lax.all_gather(arrived, 'tensor', axis=0, tiled=True)  12.1 us
    pmax x1, blocking collectives, body(): merged = lax.pmax(partial_value, 'tensor')  8.94 us
    unnamed x1, blocking collectives  7.28 us
    all_to_all x1, waiting for transfers between devices, body(): lax.all_to_all(own_best, 'dp', split_axis=0, concat_axis=0, tiled=True)  5.55 us
    all_to_all x1, starting transfers between devices, body(): lax.all_to_all(outgoing, 'dp', split_axis=0, concat_axis=0, tiled=True)  4.63 us
    all_to_all x1, starting transfers between devices, body(): lax.all_to_all(slot_tag, 'dp', split_axis=0, concat_axis=0, tiled=True)  4.6 us
  transfers between devices with their start and end apart: 5, of which 4 were waited for; matrix products, arithmetic and copies ran while one was open for 5% of the time, Pallas kernels for 0%

commit v1 on v0

v1 whole, which is shorter than its diff:
```python
import functools
import math

import jax
import jax.numpy as jnp
from jax import lax
from jax.experimental import pallas as pl
from jax.experimental.pallas import tpu as pltpu
from jax.sharding import PartitionSpec as P

EPSILON = 1e-06
MESH = pl.DeviceIdType.MESH
F32 = jnp.float32
BF16 = jnp.bfloat16
LOWEST = -1e30
CHUNKS = 2


def iota(shape, dim):
    return lax.broadcasted_iota(jnp.int32, shape, dim).astype(F32)


def to_column(row, size):
    eye = iota((size, size), 0) == iota((size, size), 1)
    return jnp.sum(jnp.where(eye, row, 0.0), axis=1, keepdims=True)


def to_row(column, size):
    eye = iota((size, size), 0) == iota((size, size), 1)
    return jnp.sum(jnp.where(eye, column, 0.0), axis=0, keepdims=True)


class Sizes:
    def __init__(self, n_dp, n_tensor, rows, hid, width, emb, members):
        self.n_dp, self.n_tensor = n_dp, n_tensor
        self.rows, self.hid, self.width, self.emb, self.members = rows, hid, width, emb, members
        self.nx = max(d for d in range(1, math.isqrt(n_tensor) + 1) if n_tensor % d == 0)
        self.ny = n_tensor // self.nx
        self.cap = min(rows, max(2, 2 * rows // n_dp))
        self.whole = self.cap // 16 * 16
        self.rest = self.cap - self.whole
        self.cols = emb // CHUNKS
        self.tiles = self.cols // 128
        self.folded = -(-self.rest * self.tiles // 16) * 16
        self.block = self.whole * self.tiles + self.folded
        self.slots = n_dp * self.cap
        self.lanes = -(-self.slots // 128) * 128


def kernel(
    z,
    features,
    w_hidden,
    w_embed,
    members,
    doc_owner,
    doc_local,
    member_cluster,
    member_valid,
    best,
    feat,
    w1,
    w2,
    raw,
    unit,
    member_tag,
    sums_out,
    sums_in,
    docs_out,
    docs_in,
    tags_out,
    tags_in,
    answer_out,
    answer_in,
    local_sem,
    feat_send,
    feat_recv,
    unit_send,
    unit_recv,
    mtag_send,
    mtag_recv,
    sums_send,
    sums_recv,
    docs_send,
    docs_recv,
    tags_send,
    tags_recv,
    answer_send,
    answer_recv,
):
    p = lax.axis_index("dp")
    t = lax.axis_index("tensor")
    tx, ty = lax.rem(t, z.nx), lax.div(t, z.nx)
    half = z.hid // 2
    sent = []

    def forward_of(j):
        dx, dy = j % z.nx, j // z.nx
        return lax.rem(ty + dy, z.ny) * z.nx + lax.rem(tx + dx, z.nx)

    def source_of(j):
        dx, dy = j % z.nx, j // z.nx
        return lax.rem(ty + z.ny - dy, z.ny) * z.nx + lax.rem(tx + z.nx - dx, z.nx)

    def remote(src, dst, send, recv, **device):
        copy = pltpu.make_async_remote_copy(
            src_ref=src, dst_ref=dst, send_sem=send, recv_sem=recv, device_id=device,
            device_id_type=MESH,
        )
        copy.start()
        sent.append(copy)
        return copy

    barrier = pltpu.get_barrier_semaphore()
    for j in range(1, z.n_tensor):
        pl.semaphore_signal(barrier, inc=1, device_id={"tensor": forward_of(j)}, device_id_type=MESH)
    for k in range(1, z.n_dp):
        pl.semaphore_signal(
            barrier, inc=1, device_id={"dp": lax.rem(p + k, z.n_dp)}, device_id_type=MESH
        )

    own = [
        pltpu.make_async_copy(features.at[:, pl.ds(h * half, half)], feat.at[h, 0], local_sem.at[h])
        for h in (0, 1)
    ]
    load_w1 = [
        pltpu.make_async_copy(
            w_hidden.at[pl.ds(h * half, half)], w1.at[pl.ds(h * half, half)], local_sem.at[2 + h]
        )
        for h in (0, 1)
    ]
    load_w2 = pltpu.make_async_copy(w_embed, w2, local_sem.at[4])
    load_members = pltpu.make_async_copy(members.at[0], raw, local_sem.at[5])
    for copy in (*own, *load_w1, load_w2, load_members):
        copy.start()

    pl.semaphore_wait(barrier, z.n_tensor - 1 + z.n_dp - 1)

    feat_copy = {}

    def send_feature(h, j, src, target):
        feat_copy[h, j] = remote(
            src, feat.at[h, j], feat_send.at[h, j], feat_recv.at[h, j], tensor=forward_of(target)
        )

    along_x = [dx for dx in range(1, z.nx)]
    along_y = [dy * z.nx for dy in range(1, z.ny)]
    for first in (0, 1):
        for j in along_x:
            h = first
            send_feature(h, j, features.at[:, pl.ds(h * half, half)], j)
        for j in along_y:
            h = 1 - first
            send_feature(h, j, features.at[:, pl.ds(h * half, half)], j)

    rows, wide = z.rows, doc_owner.shape[1]
    mine = iota((rows, wide), 1) == iota((rows, wide), 0) + (t * rows).astype(F32)
    owner = jnp.sum(jnp.where(mine, doc_owner[...].astype(F32), 0.0), axis=1, keepdims=True)
    local = jnp.sum(jnp.where(mine, doc_local[...].astype(F32), 0.0), axis=1, keepdims=True)
    step = owner - p.astype(F32)
    step = jnp.where(step < 0.0, step + float(z.n_dp), step)
    step_row = to_row(step, rows)
    same = step == step_row
    above = iota((rows, rows), 0)
    across = iota((rows, rows), 1)
    rank = jnp.sum(jnp.where(same & (across < above), 1.0, 0.0), axis=1, keepdims=True)
    rank_row = jnp.sum(jnp.where(same & (above < across), 1.0, 0.0), axis=0, keepdims=True)
    place = jnp.where(
        rank < float(z.whole),
        step * float(z.whole) + rank,
        float(z.n_dp * z.whole) + step * float(z.rest) + rank - float(z.whole),
    )
    placed = iota((rows, z.lanes), 1) == place
    step_hot = jnp.where(iota((z.n_dp, rows), 0) == step_row, 1.0, 0.0).astype(BF16)
    tags = jnp.dot(
        step_hot,
        jnp.where(placed, local + 1.0, 0.0).astype(BF16),
        preferred_element_type=F32,
    )
    for k in range(z.n_dp):
        tags_out[k] = tags[k : k + 1, :]
    tags_copy = [
        remote(
            tags_out.at[k], tags_in.at[k], tags_send.at[k], tags_recv.at[k],
            dp=lax.rem(p + k, z.n_dp),
        )
        for k in range(1, z.n_dp)
    ]

    member_tag[0] = jnp.where(
        member_valid[...] == 1, member_cluster[...].astype(F32) + 1.0, -1.0
    )
    load_members.wait()
    values = raw[...].astype(F32)
    unit[0] = (
        values / jnp.sqrt(jnp.sum(values * values, axis=1, keepdims=True) + EPSILON)
    ).astype(BF16)

    def head(j):
        total = jnp.dot(feat[0, j], w1[:half, :], preferred_element_type=F32)
        total += jnp.dot(feat[1, j], w1[half:, :], preferred_element_type=F32)
        hidden = jax.nn.gelu(total).astype(BF16)
        for c in range(CHUNKS):
            sums_out[c, j] = jnp.dot(
                hidden, w2[:, c * z.cols : (c + 1) * z.cols], preferred_element_type=F32
            ).astype(BF16)
            if j:
                sums_copy[c, j] = remote(
                    sums_out.at[c, j], sums_in.at[c, j], sums_send.at[c, j], sums_recv.at[c, j],
                    tensor=source_of(j),
                )

    sums_copy = {}
    for copy in (*own, *load_w1, load_w2):
        copy.wait()
    head(0)

    for j in along_x:
        feat_copy[0, j].wait_recv()
        for dy in along_y:
            send_feature(0, j + dy, feat.at[0, j], dy)
    for j in along_y:
        feat_copy[1, j].wait_recv()
        for dx in along_x:
            send_feature(1, j + dx, feat.at[1, j], dx)
    for j in along_x:
        feat_copy[1, j].wait_recv()
        head(j)
    for j in along_y:
        feat_copy[0, j].wait_recv()
        head(j)
    for dy in along_y:
        for dx in along_x:
            feat_copy[0, dy + dx].wait_recv()
            feat_copy[1, dy + dx].wait_recv()
            head(dy + dx)

    unit_copy = []
    for j in range(1, z.n_tensor):
        target = forward_of(j)
        unit_copy.append(
            remote(unit.at[0], unit.at[j], unit_send.at[j], unit_recv.at[j], tensor=target)
        )
        unit_copy.append(
            remote(
                member_tag.at[0], member_tag.at[j], mtag_send.at[j], mtag_recv.at[j], tensor=target
            )
        )

    code = step_row * float(z.cap) + rank_row
    code = code.reshape(1, 1, rows)
    if z.whole:
        shape = (z.n_dp, z.whole, rows)
        pack_whole = jnp.where(
            code == iota(shape, 0) * float(z.cap) + iota(shape, 1), 1.0, 0.0
        ).reshape(z.n_dp * z.whole, rows).astype(BF16)
    pack_rest = []
    if z.rest:
        shape = (z.n_dp, z.folded, rows)
        for c in range(z.tiles):
            at = iota(shape, 1) - float(c * z.rest)
            inside = (at >= 0.0) & (at < float(z.rest))
            hit = inside & (code == iota(shape, 0) * float(z.cap) + float(z.whole) + at)
            pack_rest.append(
                jnp.where(hit, 1.0, 0.0).reshape(z.n_dp * z.folded, rows).astype(BF16)
            )

    square = jnp.zeros((rows, 1), F32)
    docs_copy = {}
    for c in range(CHUNKS):
        proj = sums_out[c, 0].astype(F32)
        for j in range(1, z.n_tensor):
            sums_copy[c, j].wait_recv()
            proj += sums_in[c, j].astype(F32)
        query = proj.astype(BF16)
        if z.whole:
            packed = jnp.dot(pack_whole, query, preferred_element_type=F32).astype(BF16)
        if z.rest:
            tail = jnp.zeros((z.n_dp * z.folded, 128), F32)
            for i in range(z.tiles):
                tail += jnp.dot(
                    pack_rest[i], query[:, i * 128 : (i + 1) * 128], preferred_element_type=F32
                )
            tail = tail.astype(BF16)
        for k in [*range(1, z.n_dp), 0]:
            target = docs_out if k else docs_in
            if z.whole:
                for i in range(z.tiles):
                    target[c, k, i * z.whole : (i + 1) * z.whole, :] = packed[
                        k * z.whole : (k + 1) * z.whole, i * 128 : (i + 1) * 128
                    ]
            if z.rest:
                target[c, k, z.tiles * z.whole :, :] = tail[k * z.folded : (k + 1) * z.folded, :]
            if k:
                docs_copy[c, k] = remote(
                    docs_out.at[c, k], docs_in.at[c, k], docs_send.at[c, k], docs_recv.at[c, k],
                    dp=lax.rem(p + k, z.n_dp),
                )
        square += jnp.sum(proj * proj, axis=1, keepdims=True)
    inverse = 1.0 / jnp.sqrt(square + EPSILON)

    tag_row = tags_out[0]
    for k in range(1, z.n_dp):
        tags_copy[k - 1].wait_recv()
        tag_row += tags_in[k]
    tag_row = tag_row[:, : z.slots]
    for copy in unit_copy:
        copy.wait_recv()
    allowed = [to_column(member_tag[j], z.members) for j in range(z.n_tensor)]

    unfold = []
    if z.rest:
        shape = (z.n_dp * z.rest, z.n_dp * z.folded)
        out_row, in_row = iota(shape, 0), iota(shape, 1)
        for i in range(z.tiles):
            hit = jnp.zeros(shape, F32)
            for k in range(z.n_dp):
                at = out_row - float(k * z.rest)
                inside = (at >= 0.0) & (at < float(z.rest))
                hit = jnp.where(
                    inside & (in_row == at + float(k * z.folded + i * z.rest)), 1.0, hit
                )
            unfold.append(hit.astype(BF16))

    scores = [jnp.zeros((z.members, z.slots), F32) for _ in range(z.n_tensor)]
    for c in range(CHUNKS):
        for k in range(1, z.n_dp):
            docs_copy[c, k].wait_recv()
        parts = []
        if z.whole:
            parts.append(
                jnp.concatenate(
                    [
                        docs_in[c, :, i * z.whole : (i + 1) * z.whole, :].reshape(
                            z.n_dp * z.whole, 128
                        )
                        for i in range(z.tiles)
                    ],
                    axis=1,
                )
            )
        if z.rest:
            tail = docs_in[c, :, z.tiles * z.whole :, :].reshape(z.n_dp * z.folded, 128)
            parts.append(
                jnp.concatenate(
                    [
                        jnp.dot(unfold[i], tail, preferred_element_type=F32).astype(BF16)
                        for i in range(z.tiles)
                    ],
                    axis=1,
                )
            )
        arrived = jnp.concatenate(parts, axis=0) if len(parts) > 1 else parts[0]
        for j in range(z.n_tensor):
            scores[j] += lax.dot_general(
                unit[j, :, c * z.cols : (c + 1) * z.cols],
                arrived,
                (((1,), (1,)), ((), ())),
                preferred_element_type=F32,
            )
    top = jnp.full((1, z.slots), LOWEST, F32)
    for j in range(z.n_tensor):
        kept = jnp.where(allowed[j] == tag_row, scores[j], LOWEST)
        top = jnp.maximum(top, jnp.max(kept, axis=0, keepdims=True))
    answer_out[...] = jnp.zeros_like(answer_out)
    answer_out[:, : z.slots] = top

    answer_copy = [
        remote(
            answer_out, answer_in.at[k], answer_send.at[k], answer_recv.at[k],
            dp=lax.rem(p + z.n_dp - k, z.n_dp),
        )
        for k in range(1, z.n_dp)
    ]
    found = jnp.where(step == 0.0, answer_out[...], 0.0)
    for k in range(1, z.n_dp):
        answer_copy[k - 1].wait_recv()
        found = jnp.where(step == float(k), answer_in[k], found)
    value = jnp.sum(jnp.where(placed, found, 0.0), axis=1, keepdims=True)
    best[...] = to_row(jnp.maximum(value * inverse, -1.0), rows)
    for copy in sent:
        copy.wait_send()


def body(features, w_hidden, w_embed, members, doc_owner, doc_local, member_cluster, member_valid):
    n_dp, n_tensor = lax.axis_size("dp"), lax.axis_size("tensor")
    rows, hid = features.shape
    width, emb = w_embed.shape
    z = Sizes(n_dp, n_tensor, rows, hid, width, emb, members.shape[1])
    half = hid // 2
    dma = pltpu.SemaphoreType.DMA
    hbm = pl.BlockSpec(memory_space=pl.ANY)
    vmem = pl.BlockSpec(memory_space=pltpu.VMEM)
    out = pl.pallas_call(
        functools.partial(kernel, z),
        out_shape=jax.ShapeDtypeStruct((1, rows), F32),
        in_specs=[hbm] * 4 + [vmem] * 4,
        out_specs=vmem,
        scratch_shapes=[
            pltpu.VMEM((2, n_tensor, rows, half), BF16),
            pltpu.VMEM((hid, width), BF16),
            pltpu.VMEM((width, emb), BF16),
            pltpu.VMEM((z.members, emb), BF16),
            pltpu.VMEM((n_tensor, z.members, emb), BF16),
            pltpu.VMEM((n_tensor, 1, z.members), F32),
            pltpu.VMEM((CHUNKS, n_tensor, rows, z.cols), BF16),
            pltpu.VMEM((CHUNKS, n_tensor, rows, z.cols), BF16),
            pltpu.VMEM((CHUNKS, n_dp, z.block, 128), BF16),
            pltpu.VMEM((CHUNKS, n_dp, z.block, 128), BF16),
            pltpu.VMEM((n_dp, 1, z.lanes), F32),
            pltpu.VMEM((n_dp, 1, z.lanes), F32),
            pltpu.VMEM((1, z.lanes), F32),
            pltpu.VMEM((n_dp, 1, z.lanes), F32),
            dma((6,)),
            dma((2, n_tensor)),
            dma((2, n_tensor)),
            dma((n_tensor,)),
            dma((n_tensor,)),
            dma((n_tensor,)),
            dma((n_tensor,)),
            dma((CHUNKS, n_tensor)),
            dma((CHUNKS, n_tensor)),
            dma((CHUNKS, n_dp)),
            dma((CHUNKS, n_dp)),
            dma((n_dp,)),
            dma((n_dp,)),
            dma((n_dp,)),
            dma((n_dp,)),
        ],
        compiler_params=pltpu.CompilerParams(
            collective_id=0, has_side_effects=True, vmem_limit_bytes=48 * 1024 * 1024
        ),
        name="match",
    )(
        features,
        w_hidden,
        w_embed,
        members,
        doc_owner.reshape(1, -1),
        doc_local.reshape(1, -1),
        member_cluster,
        member_valid,
    )
    return out.reshape(rows)


def solution(mesh):
    return jax.shard_map(
        body,
        mesh=mesh,
        in_specs=(
            P(("dp", "tensor"), None),
            P(None, "tensor"),
            P("tensor", None),
            P("dp", "tensor", None),
            P("dp", None),
            P("dp"),
            P("dp", "tensor"),
            P("dp", "tensor"),
        ),
        out_specs=P(("dp", "tensor")),
        check_vma=False,
    )
```

time: 129 us -> 45.4 us (0.35)
  waiting for transfers between devices: 57.3 us -> 0 us
  Pallas kernels: 0 us -> 37.3 us
  blocking collectives: 28.3 us -> 0 us
  between operations: 14.2 us -> 0.02 us
  starting transfers between devices: 13 us -> 0 us
  matrix products: 5.25 us -> 0 us
  other arithmetic: 4.4 us -> 0 us
  local copies, waits for them, and re-layouts: 6.32 us -> 7.81 us
    pallas_call x0 -> x1, Pallas kernels: none -> 37.3 us  [body(): pl.pallas_call(functools.partial(kernel, z), out_shape=jax.ShapeDtypeStru...]
    all_gather x1 -> x0, waiting for transfers between devices: 32.3 us -> none  [body(): lax.all_gather(features, 'tensor', axis=0, tiled=True)]
    reduce_scatter x1 -> x0, waiting for transfers between devices: 17.1 us -> none  [body(): lax.psum_scatter(jnp.dot(hidden, w_embed, preferred_element_type=jnp.floa...]
    all_to_all x3 -> x0, starting transfers between devices: 13 us -> none  [the longest x1 4.63 us: body(): lax.all_to_all(outgoing, 'dp', split_axis=0, concat_axis=0, tiled=True)]
    all_gather x1 -> x0, blocking collectives: 12.1 us -> none  [body(): lax.all_gather(arrived, 'tensor', axis=0, tiled=True)]
    pmax x1 -> x0, blocking collectives: 8.94 us -> none  [body(): merged = lax.pmax(partial_value, 'tensor')]
    unnamed x1 -> x0, blocking collectives: 7.28 us -> none
    all_to_all x3 -> x0, waiting for transfers between devices: 7.19 us -> none  [the longest x1 5.55 us: body(): lax.all_to_all(own_best, 'dp', split_axis=0, concat_axis=0, tiled=True)]
  transfers between devices with their start and end apart: 5 -> 0, of which waited for: 4 -> 0; matrix products, arithmetic and copies ran while one was open for 5% -> 0% of each run, Pallas kernels for 0% -> 0%
where the time goes in v1:
time: 45.4 us; the launch traced here: 45.1 us
  Pallas kernels  37.3 us (82%)
  local copies, waits for them, and re-layouts  7.81 us (17%)
    pallas_call x1, Pallas kernels, body(): pl.pallas_call(functools.partial(kernel, z), out_shape=jax.ShapeDtypeStru...  37.3 us
    unnamed x15, local copies, waits for them, and re-layouts  7.12 us

profile of v1, /device:TPU:0, one launch (start us, length us, event | category | flops | bytes accessed | tf_op | source)
XLA Modules:
  0.0 45.1 jit_solution(6973960315150064206)
XLA Ops:
  0.0 0.7 %reshape.10.doc_local = s32[1,320]{1,0:T(1,128)S(1)} reshape(s32[320]{0:T(512)} %param.13) | data formatting | bytes 2560 | tf_op jit(solution)/shard_map/reshape | solution.py:440
  0.7 0.0 copy-start
  0.7 1.6 %copy-done = bf16[2048,512]{1,0:T(8,128)(2,1)S(1)} copy-done((bf16[2048,512]{1,0:T(8,128)(2,1)S(1)}, bf16[2048,512]{1,0:T(8,128)(2,1)}, u32[]{:S(2)}) %copy-start) | copy-done | bytes 2097176
  2.3 0.0 copy-start.1
  2.3 1.1 %copy-done.1 = bf16[512,768]{1,0:T(8,128)(2,1)S(1)} copy-done((bf16[512,768]{1,0:T(8,128)(2,1)S(1)}, bf16[512,768]{1,0:T(8,128)(2,1)}, u32[]{:S(2)}) %copy-start.1) | copy-done | bytes 786456
  3.4 0.0 copy-start.2
  3.4 1.0 %copy-done.2 = bf16[80,2048]{1,0:T(8,128)(2,1)S(1)} copy-done((bf16[80,2048]{1,0:T(8,128)(2,1)S(1)}, bf16[80,2048]{1,0:T(8,128)(2,1)}, u32[]{:S(2)}) %copy-start.2) | copy-done | bytes 327704
  4.4 0.0 copy-start.3
  4.4 0.9 %copy-done.3 = bf16[1,128,768]{2,1,0:T(8,128)(2,1)S(1)} copy-done((bf16[1,128,768]{2,1,0:T(8,128)(2,1)S(1)}, bf16[1,128,768]{2,1,0:T(8,128)(2,1)}, u32[]{:S(2)}) %copy-start.3) | copy-done | bytes 196632
  5.3 0.0 copy-start.4
  5.3 0.7 %copy-done.4 = s32[320,1]{0,1:T(1,128)S(1)} copy-done((s32[320,1]{0,1:T(1,128)S(1)}, s32[320,1]{0,1:T(1,128)}, u32[]{:S(2)}) %copy-start.4) | copy-done | bytes 1304
  6.0 0.0 copy-start.5
  6.0 0.7 %copy-done.5 = s32[1,128]{1,0:T(1,128)S(1)} copy-done((s32[1,128]{1,0:T(1,128)S(1)}, s32[1,128]{1,0:T(1,128)}, u32[]{:S(2)}) %copy-start.5) | copy-done | bytes 536
  6.6 0.0 copy-start.6
  6.6 0.7 %copy-done.6 = s32[1,128]{1,0:T(1,128)S(1)} copy-done((s32[1,128]{1,0:T(1,128)S(1)}, s32[1,128]{1,0:T(1,128)}, u32[]{:S(2)}) %copy-start.6) | copy-done | bytes 536
  7.3 37.3 %match.1 = f32[1,80]{1,0:T(1,128)S(1)} custom-call(bf16[80,2048]{1,0:T(8,128)(2,1)S(1)} %copy-done.2, bf16[2048,512]{1,0:T(8,128)(2,1)S(1)} %copy-done, bf16[512,768]{1,0:T(8,128)(2,1)S(1)} %copy-done.1, bf16[1,128,768]{2,1,0:T(8,128)(2,1)S(1)} %copy-done.3, s32[1,320]{1,0:T(1,128)S(1)} %bitcast.2, s32[1,320]{1,0:T(1,128)S(1)} %reshape.10.doc_local, ...), custom_call_target="tpu_custom_call" | custom-call | tf_op jit(solution)/shard_map/match/pallas_call | solution.py:394
  44.6 0.5 %copy.10 = f32[80]{0:T(128)} copy(f32[80]{0:T(128)S(1)} %bitcast.3) | data formatting | bytes 640
Async XLA Ops:
  0.7 1.6 %copy-start = (bf16[2048,512]{1,0:T(8,128)(2,1)S(1)}, bf16[2048,512]{1,0:T(8,128)(2,1)}, u32[]{:S(2)}) copy-start(bf16[2048,512]{1,0:T(8,128)(2,1)} %w_hidden.1) | copy-start | bytes 6291460
  2.3 1.1 %copy-start.1 = (bf16[512,768]{1,0:T(8,128)(2,1)S(1)}, bf16[512,768]{1,0:T(8,128)(2,1)}, u32[]{:S(2)}) copy-start(bf16[512,768]{1,0:T(8,128)(2,1)} %w_embed.1) | copy-start | bytes 2359300
  3.4 1.0 %copy-start.2 = (bf16[80,2048]{1,0:T(8,128)(2,1)S(1)}, bf16[80,2048]{1,0:T(8,128)(2,1)}, u32[]{:S(2)}) copy-start(bf16[80,2048]{1,0:T(8,128)(2,1)} %features.1) | copy-start | bytes 983044
  4.4 0.9 %copy-start.3 = (bf16[1,128,768]{2,1,0:T(8,128)(2,1)S(1)}, bf16[1,128,768]{2,1,0:T(8,128)(2,1)}, u32[]{:S(2)}) copy-start(bf16[1,128,768]{2,1,0:T(8,128)(2,1)} %members.1) | copy-start | bytes 589828
  5.3 0.7 %copy-start.4 = (s32[320,1]{0,1:T(1,128)S(1)}, s32[320,1]{0,1:T(1,128)}, u32[]{:S(2)}) copy-start(s32[320,1]{0,1:T(1,128)} %param.12) | copy-start | bytes 3844
  6.0 0.7 %copy-start.5 = (s32[1,128]{1,0:T(1,128)S(1)}, s32[1,128]{1,0:T(1,128)}, u32[]{:S(2)}) copy-start(s32[1,128]{1,0:T(1,128)} %member_cluster.1) | copy-start | bytes 1540
  6.6 0.7 %copy-start.6 = (s32[1,128]{1,0:T(1,128)S(1)}, s32[1,128]{1,0:T(1,128)}, u32[]{:S(2)}) copy-start(s32[1,128]{1,0:T(1,128)} %member_valid.1) | copy-start | bytes 1540
